TPU v7x, 256 devices: a whole 4x4x8 slice. The times are simulated.
256 devices in a mesh: phase: 4 (over x), dp: 16 (over z, core), fsdp: 4 (over y).
Axes of the slice: x: 4, y: 4, z: 8, core: 2. Of those that a mesh axis runs over, the one named last changes fastest.
Arguments:
- audio_frames: bfloat16 [16384, 1280], P(('dp', 'fsdp')), may hold values from -6 to 6
- vision_patches: bfloat16 [16384, 1280], P(('dp', 'fsdp')), may hold values from -6 to 6
- audio_blocks: int32 [64, 256], P(('dp', 'fsdp')), may hold values from 0 to 7, never falling along the last dimension, each value on 1 to 128 neighbouring positions
- vision_windows: int32 [64, 256], P(('dp', 'fsdp')), may hold values from 0 to 7, never falling along the last dimension, each value on 1 to 112 neighbouring positions
- insert_order: int32 [64, 768], P(('dp', 'fsdp')), may hold values from 0 to 767, each once within a row
- text_embeds: bfloat16 [49152, 8192], P(('dp', 'fsdp'), 'phase'), may hold values from -6 to 6
- ln_gain: bfloat16 [4, 1280], P('phase'), may hold values from 0.5 to 1.5
- attn_qkv: bfloat16 [4, 1280, 3840], P('phase', ('dp', 'fsdp')), may hold values from -1 to 1
- attn_out: bfloat16 [4, 1280, 1280], P('phase', ('dp', 'fsdp')), may hold values from -0.15625 to 0.15625
- projector: bfloat16 [1280, 8192], P(('dp', 'fsdp'), 'phase'), may hold values from -0.15625 to 0.15625
Outputs:
- llm_rows: bfloat16 [49152, 8192], P(('dp', 'fsdp'), 'phase')
Inputs may be any that keep to these rules, and one draw needn't show every extreme that they name: `audio_blocks`: each row never falls, each block holds 1 to 128 frames, one exactly 128. `vision_windows`: each row never falls, each window holds 1 to 112 patches, one exactly 112. `insert_order`: each row is a permutation of 0 to 767.
All inputs are finite; a program needn't handle non-finite values.
Results may differ from a plain program's by a relative error of at most 0.012.
The roundings to bfloat16 on the way count: a program that leaves them out, or rounds other values in their place, can miss the bound.
Values may be sent and summed in bfloat16 or wider, within the bound.
A program may use at most 192 MiB of HBM per device.

v0:
```python
import jax
import jax.numpy as jnp
from jax import lax
from jax.sharding import PartitionSpec as P


def shifted(shard, axis, by):
    peers = lax.axis_size(axis)
    pairs = [(i, i + by) for i in range(peers) if 0 <= i + by < peers]
    return lax.ppermute(shard, axis, pairs)


def broadcast(value, axis, source):
    kept = jnp.where(lax.axis_index(axis) == source, value, 0).astype(value.dtype)
    return lax.psum(kept, axis)


def norm_rows(input_rows, gain_vec):
    values = input_rows.astype(jnp.float32)
    centre = values - jnp.mean(values, axis=-1, keepdims=True)
    spread = jnp.mean(centre * centre, axis=-1, keepdims=True)
    return (centre * lax.rsqrt(spread + 1e-05) * gain_vec.astype(jnp.float32)).astype(jnp.bfloat16)


def attention_core(query, keys, values, ids_query, ids_keys, head_count):
    row_count, model_width = query.shape
    head_size = model_width // head_count
    query_heads = query.reshape(row_count, head_count, head_size)
    key_heads = keys.reshape(-1, head_count, head_size)
    value_heads = values.reshape(-1, head_count, head_size)
    scores = jnp.einsum("qhd,khd->hqk", query_heads, key_heads, preferred_element_type=jnp.float32)
    scores = scores * head_size ** (-0.5)
    same_block = ids_query[:, None] == ids_keys[None, :]
    scores = jnp.where(same_block[None], scores, -1e30)
    row_max = jnp.max(scores, axis=-1, keepdims=True)
    exponent = jnp.exp(scores - row_max)
    weights = (exponent / jnp.sum(exponent, axis=-1, keepdims=True)).astype(jnp.bfloat16)
    mixed_rows = jnp.einsum(
        "hqk,khd->qhd", weights, value_heads, preferred_element_type=jnp.float32
    )
    return mixed_rows.reshape(row_count, model_width).astype(jnp.bfloat16)


def finish_layer(input_rows, mixed_rows, w_out):
    update = jnp.dot(mixed_rows, w_out, preferred_element_type=jnp.float32)
    return (input_rows.astype(jnp.float32) + update).astype(jnp.bfloat16)


def per_device(
    audio_frames,
    vision_patches,
    audio_blocks,
    vision_windows,
    insert_order,
    text_embeds,
    ln_gain,
    attn_qkv,
    attn_out,
    projector,
):
    phase_index = lax.axis_index("phase")
    audio_side = phase_index < 2
    is_second = phase_index % 2 == 1
    row_count, model_width = audio_frames.shape
    source_rows = jnp.where(audio_side, audio_frames, vision_patches)
    block_ids = jnp.where(audio_side, audio_blocks[0], vision_windows[0])
    heads_audio = model_width // 64
    heads_vision = model_width // 80

    def attend(query, keys, values, ids_query):
        return lax.cond(
            audio_side,
            lambda: attention_core(query, keys, values, ids_query, block_ids, heads_audio),
            lambda: attention_core(query, keys, values, ids_query, block_ids, heads_vision),
        )

    own_qkv, own_out = (
        lax.all_gather(attn_qkv[0], ("dp", "fsdp"), axis=0, tiled=True),
        lax.all_gather(attn_out[0], ("dp", "fsdp"), axis=0, tiled=True),
    )

    def full_layer(input_rows):
        normed = norm_rows(input_rows, ln_gain[0])
        packed = jnp.dot(normed, own_qkv, preferred_element_type=jnp.float32).astype(jnp.bfloat16)
        mixed_rows = attend(
            packed[:, :model_width],
            packed[:, model_width : 2 * model_width],
            packed[:, 2 * model_width :],
            block_ids,
        )
        return finish_layer(input_rows, mixed_rows, own_out)

    zero_rows = jnp.zeros_like(source_rows)
    after_first = lax.cond(is_second, lambda: zero_rows, lambda: full_layer(source_rows))
    handed_rows = shifted(after_first, "phase", 1)
    encoded = lax.cond(is_second, lambda: full_layer(handed_rows), lambda: zero_rows)
    audio_done = broadcast(encoded, "phase", 1)
    vision_done = broadcast(encoded, "phase", 3)
    encoded_rows = jnp.concatenate([audio_done, vision_done], axis=0)
    projected = jnp.dot(
        encoded_rows,
        lax.all_gather(projector, ("dp", "fsdp"), axis=0, tiled=True),
        preferred_element_type=jnp.float32,
    )
    projected = projected.astype(jnp.bfloat16)
    return text_embeds.at[insert_order[0, : 2 * row_count]].set(projected)


def solution(mesh):
    placed = (
        P(("dp", "fsdp"), None),
        P(("dp", "fsdp"), None),
        P(("dp", "fsdp"), None),
        P(("dp", "fsdp"), None),
        P(("dp", "fsdp"), None),
        P(("dp", "fsdp"), "phase"),
        P("phase", None),
        P("phase", ("dp", "fsdp"), None),
        P("phase", ("dp", "fsdp"), None),
        P(("dp", "fsdp"), "phase"),
    )
    return jax.shard_map(
        per_device,
        mesh=mesh,
        in_specs=placed,
        out_specs=P(("dp", "fsdp"), "phase"),
        check_vma=False,
    )
```

profile of v0, /device:TPU:4, one launch (start us, length us, event | category | flops | bytes accessed | tf_op | source)
XLA Modules:
  0.0 354.2 jit_solution(2293237445071210810)
XLA Ops:
  6.5 0.0 copy-start.6
  6.5 0.0 copy-start.7
  6.5 0.0 copy-start.2
  6.5 0.0 copy-start.3
  6.5 0.0 all-gather.9.cloned.1.call-start
  6.6 4.0 %copy.63 = bf16[768,2048]{1,0:T(8,128)(2,1)} copy(bf16[768,2048]{1,0:T(8,128)(2,1)} %param.23) | data formatting | bytes 6291456
  10.6 0.0 copy-done.3
  10.6 0.7 copy.40
  11.3 0.0 all-gather.9.cloned.1.call-update
  11.3 0.0 all-gather.7.cloned.1.call-start
  11.4 0.0 copy-done.2
  11.4 1.0 copy.39
  12.3 0.0 all-gather.7.cloned.1.call-update
  12.4 0.0 all-gather.11.cloned.1.call-start
  12.4 0.7 all-gather.11.cloned.1.call-update
  13.1 0.0 all-reduce.3.cloned.1.call-start
  13.2 0.0 copy-done.6
  13.2 0.0 copy-done.7
  13.2 82.6 %all-gather.9.cloned.1.call-done = bf16[1,1280,1280]{2,0,1:T(2,128)(2,1)} async-done(((bf16[1,20,1280]{2,0,1:T(2,128)(2,1)}), bf16[1,1280,1280]{2,0,1:T(2,128)(2,1)}) %all-gather.9.cloned.1.call-update) | async-done | bytes 3276816 | tf_op jit(solution)/shard_map/all_gather | solution.py:79
  95.8 5.1 %copy.50 = bf16[1,1280,1280]{2,1,0:T(8,128)(2,1)} copy(bf16[1,1280,1280]{2,0,1:T(2,128)(2,1)} %all-gather.9.cloned.1.call-done) | data formatting | bytes 6553600
  101.0 101.3 %all-gather.7.cloned.1.call-done = bf16[1,1280,3840]{2,0,1:T(2,128)(2,1)} async-done(((bf16[1,20,3840]{2,0,1:T(2,128)(2,1)}), bf16[1,1280,3840]{2,0,1:T(2,128)(2,1)}) %all-gather.7.cloned.1.call-update) | async-done | bytes 9830416 | tf_op jit(solution)/shard_map/all_gather | solution.py:78
  202.2 14.2 %copy.49 = bf16[1,1280,3840]{2,1,0:T(8,128)(2,1)} copy(bf16[1,1280,3840]{2,0,1:T(2,128)(2,1)} %all-gather.7.cloned.1.call-done) | data formatting | bytes 19660800
  216.5 0.0 copy-done
  216.5 0.0 copy-done.1
  216.5 0.0 copy-done.4
  216.5 20.6 %conditional.14 = (bf16[256,1280]{1,0:T(8,128)(2,1)S(1)}) conditional(s32[]{:T(128)} %convert_element_type.106, (pred[]{:T(512)}, pred[]{:T(512)}, bf16[1,1280]{1,0:T(2,128)(2,1)S(1)}, bf16[1280,3840]{1,0:T(8,128)(2,1)}, s32[256]{0:T(256)S(1)}, /*index=5*/bf16[1280,1280]{1,0:T(8,128)(2,1)}, bf16[256,1280]{1,0:T(8,128)(2,1)S(1)}, ...), branch_computations={%region_0.9_spmd, %region_9.10_spmd} | conditional | flops 3705145088 | bytes 41482792 | solution.py:94
  216.5 0.3 convert_reduce_fusion
  216.8 0.3 fusion.47
  217.1 6.6 %convolution_convert_fusion = bf16[256,3840]{1,0:T(8,128)(2,1)S(1)} fusion(bf16[1280,3840]{1,0:T(8,128)(2,1)} %get-tuple-element.97, bf16[256,1280]{1,0:T(8,128)(2,1)S(1)} %get-tuple-element.136, f32[1280]{0:T(1024)S(1)} %convert_reduce_fusion.1, f32[256]{0:T(256)S(1)} %add_rsqrt_fusion, f32[256]{0:T(256)S(1)} %broadcast_multiply_fusion), kind=kOutput, calls=%fused_computation.57 | convolution fusion | flops 2519203840 | bytes 12459008 | tf_op jit(solution)/shard_map/cond/branch_0_fun/dot_general | solution.py:84
  223.8 10.2 %conditional.7 = (bf16[256,1280]{0,1:T(8,128)(2,1)S(1)}) conditional(s32[]{:T(128)} %convert_element_type.87, (s32[256]{0:T(256)S(1)}, bf16[256,3840]{1,0:T(8,128)(2,1)S(1)}) %tuple.41, (s32[256]{0:T(256)S(1)}, bf16[256,3840]{1,0:T(8,128)(2,1)S(1)}) %tuple.41), branch_computations={%region_3.5_spmd, %region_6.8_spmd} | conditional | flops 343802112 | bytes 21144584
  223.8 2.3 copy.33
  226.1 1.6 fusion.68
  227.7 0.1 broadcast_compare_fusion
  227.8 3.4 fusion.69
  231.2 2.7 fusion.6
  233.9 3.0 fusion.44
  237.1 1.9 collective-permute-start
  239.1 16.9 %collective-permute-done = bf16[256,1280]{1,0:T(8,128)(2,1)S(1)} collective-permute-done((bf16[256,1280]{1,0:T(8,128)(2,1)S(1)}, bf16[256,1280]{1,0:T(8,128)(2,1)S(1)}, u32[]{:S(2)}, u32[]{:S(2)}) %collective-permute-start) | collective-permute-done | bytes 655392 | tf_op jit(solution)/shard_map/ppermute | solution.py:10
  255.9 0.3 conditional.15
  256.2 0.0 copy-start.5
  256.2 1.1 broadcast_select_fusion.2
  257.4 0.0 all-reduce.3.cloned.1.call-update
  257.4 0.0 copy-done.5
  257.4 25.6 %all-gather.11.cloned.1.call-done = bf16[64,20,2048]{2,1,0:T(8,128)(2,1)} async-done(((bf16[1,20,2048]{2,1,0:T(8,128)(2,1)}), bf16[64,20,2048]{2,1,0:T(8,128)(2,1)}) %all-gather.11.cloned.1.call-update) | async-done | bytes 5242896 | tf_op jit(solution)/shard_map/all_gather | solution.py:102
  283.0 9.0 %reshape.227 = bf16[1280,2048]{1,0:T(8,128)(2,1)} reshape(bf16[64,20,2048]{2,1,0:T(8,128)(2,1)} %all-gather.11.cloned.1.call-done) | data formatting | bytes 10485760
  292.0 42.3 %all-reduce.3.cloned.1.call-done = (bf16[256,1280]{1,0:T(8,128)(2,1)}, bf16[256,1280]{1,0:T(8,128)(2,1)}) async-done(((bf16[256,1280]{1,0:T(8,128)(2,1)}, bf16[256,1280]{1,0:T(8,128)(2,1)}), (bf16[256,1280]{1,0:T(8,128)(2,1)}, bf16[256,1280]{1,0:T(8,128)(2,1)})) %all-reduce.3.cloned.1.call-update) | async-done | bytes 1310736 | tf_op jit(solution)/shard_map/psum | solution.py:15
  334.3 5.8 %convolution_convert_fusion.2 = bf16[512,2048]{1,0:T(8,128)(2,1)S(1)} fusion(bf16[1280,2048]{1,0:T(8,128)(2,1)} %reshape.227, bf16[256,1280]{1,0:T(8,128)(2,1)} %get-tuple-element.133, bf16[256,1280]{1,0:T(8,128)(2,1)} %get-tuple-element.134), kind=kOutput, calls=%fused_computation.92 | convolution fusion | flops 2688024576 | bytes 8650752 | tf_op jit(solution)/shard_map/dot_general | solution.py:100
  340.1 7.6 %scatter_fusion = bf16[768,2048]{1,0:T(8,128)(2,1)} fusion(bf16[768,2048]{1,0:T(8,128)(2,1)} %copy.63, s32[512]{0:T(512)S(1)} %bitcast.79, bf16[512,2048]{1,0:T(8,128)(2,1)S(1)} %convolution_convert_fusion.2), kind=kCustom, calls=%fused_computation | custom fusion | bytes 6293504 | tf_op jit(solution)/shard_map/scatter | solution.py:106
  (9 shorter events, 0.1 us)
Async XLA Ops:
  6.5 6.6 %copy-start.6 = (s32[1,256]{1,0:T(1,128)S(1)}, s32[1,256]{1,0:T(1,128)}, u32[]{:S(2)}) copy-start(s32[1,256]{1,0:T(1,128)} %param.20) | copy-start | bytes 3076
  6.5 6.6 %copy-start.7 = (s32[1,256]{1,0:T(1,128)S(1)}, s32[1,256]{1,0:T(1,128)}, u32[]{:S(2)}) copy-start(s32[1,256]{1,0:T(1,128)} %param.21) | copy-start | bytes 3076
  6.5 4.8 %copy-start.2 = (bf16[1,20,3840]{2,1,0:T(8,128)(2,1)S(1)}, bf16[1,20,3840]{2,1,0:T(8,128)(2,1)}, u32[]{:S(2)}) copy-start(bf16[1,20,3840]{2,1,0:T(8,128)(2,1)} %param.25) | copy-start | bytes 460804
  6.5 4.1 %copy-start.3 = (bf16[1,20,1280]{2,1,0:T(8,128)(2,1)S(1)}, bf16[1,20,1280]{2,1,0:T(8,128)(2,1)}, u32[]{:S(2)}) copy-start(bf16[1,20,1280]{2,1,0:T(8,128)(2,1)} %param.26) | copy-start | bytes 153604
  6.5 89.3 %all-gather.9.cloned.1.call-start = ((), (), s32[]{:S(2)}) async-start(), calls=%async_computation.1 | async-start | bytes 6656000 | tf_op jit(solution)/shard_map/all_gather | solution.py:79
  11.3 190.9 %all-gather.7.cloned.1.call-start = ((), (), s32[]{:S(2)}) async-start(), calls=%async_computation | async-start | bytes 19968000 | tf_op jit(solution)/shard_map/all_gather | solution.py:78
  12.4 270.6 %all-gather.11.cloned.1.call-start = ((), (), s32[]{:S(2)}) async-start(), calls=%async_computation.2 | async-start | bytes 6389760 | tf_op jit(solution)/shard_map/all_gather | solution.py:102
  13.1 321.2 %all-reduce.3.cloned.1.call-start = ((), (), s32[]{:S(2)}) async-start(), calls=%async_computation.3 | async-start | bytes 2621440 | tf_op jit(solution)/shard_map/psum | solution.py:15
  101.0 115.5 %copy-start = (bf16[256,1280]{1,0:T(8,128)(2,1)S(1)}, bf16[256,1280]{1,0:T(8,128)(2,1)}, u32[]{:S(2)}) copy-start(bf16[256,1280]{1,0:T(8,128)(2,1)} %param.18) | copy-start | bytes 1966084
  101.0 115.5 %copy-start.1 = (bf16[256,1280]{1,0:T(8,128)(2,1)S(1)}, bf16[256,1280]{1,0:T(8,128)(2,1)}, u32[]{:S(2)}) copy-start(bf16[256,1280]{1,0:T(8,128)(2,1)} %param.19) | copy-start | bytes 1966084
  101.0 115.5 %copy-start.4 = (bf16[1,1280]{1,0:T(2,128)(2,1)S(1)}, bf16[1,1280]{1,0:T(2,128)(2,1)}, u32[]{:S(2)}) copy-start(bf16[1,1280]{1,0:T(2,128)(2,1)} %param.24) | copy-start | bytes 7684
  237.1 18.8 %collective-permute-start = (bf16[256,1280]{1,0:T(8,128)(2,1)S(1)}, bf16[256,1280]{1,0:T(8,128)(2,1)S(1)}, u32[]{:S(2)}, u32[]{:S(2)}) collective-permute-start(bf16[256,1280]{1,0:T(8,128)(2,1)S(1)} %get-tuple-element.163), channel_id=1, source_target_pairs={{0,64},{64,128},{128,192},{1,65},{65,129},{129,193},{2,66},{66,130... | collective-permute-start | bytes 1966088 | tf_op jit(solution)/shard_map/ppermute | solution.py:10
  256.2 1.2 copy-start.5
Sparse Core Ops, SparseCore 0:
  11.4 84.3 all-gather.8
  98.5 103.6 all-gather.6
  205.0 77.9 all-gather.10
  285.2 49.0 all-reduce.2
where the time goes:
time: 355 us; the launch traced here: 354 us
  waiting for transfers between devices  269 us (76%)
  local copies, waits for them, and re-layouts  45.6 us (13%)
  matrix products  21.5 us (6%)
  between operations  13.3 us (4%)
    all_gather x1, waiting for transfers between devices, per_device(): lax.all_gather(attn_qkv[0], ('dp', 'fsdp'), axis=0, tiled=True)  101 us
    all_gather x1, waiting for transfers between devices, per_device(): lax.all_gather(attn_out[0], ('dp', 'fsdp'), axis=0, tiled=True)  82.6 us
    psum x1, waiting for transfers between devices, broadcast(): return lax.psum(kept, axis)  42.3 us
    unnamed x22, local copies, waits for them, and re-layouts  34.1 us
    all_gather x1, waiting for transfers between devices, per_device(): lax.all_gather(projector, ('dp', 'fsdp'), axis=0, tiled=True)  25.6 us
    ppermute x1, waiting for transfers between devices, shifted(): return lax.ppermute(shard, axis, pairs)  16.9 us
    scatter x1, local copies, waits for them, and re-layouts, per_device(): return text_embeds.at[insert_order[0, :2 * row_count]].set(projected)  7.57 us
  transfers between devices with their start and end apart: 5, of which 5 were waited for; matrix products, arithmetic and copies ran while one was open for 14% of the time, Pallas kernels for 0%

commit v1 on v0

v1 whole, which is shorter than its diff:
```python
import jax
import jax.numpy as jnp
from jax import lax
from jax.experimental import pallas as pl
from jax.experimental.pallas import tpu as pltpu
from jax.sharding import PartitionSpec as P

MESH = pl.DeviceIdType.MESH
BF = jnp.bfloat16
F32 = jnp.float32
ROWS = 256
HALF = 640
N_COPIES = 300


class Copies:
    def __init__(self, send, recv):
        self.send, self.recv, self.made = send, recv, []

    def start(self, src, dst, to):
        at = len(self.made)
        copy = pltpu.make_async_remote_copy(
            src_ref=src,
            dst_ref=dst,
            send_sem=self.send.at[at],
            recv_sem=self.recv.at[at],
            device_id=to,
            device_id_type=MESH,
        )
        copy.start()
        self.made.append(copy)
        return copy

    def finish(self):
        for copy in self.made:
            if copy is not None:
                copy.wait_send()

    def wait(self, copy):
        copy.wait()
        self.made = [None if other is copy else other for other in self.made]


class Place:
    def __init__(self):
        self.p = lax.axis_index("phase")
        self.d = lax.axis_index("dp")
        self.y = lax.axis_index("fsdp")
        self.z = self.d // 2
        self.c = self.d % 2

    def z_at(self, k):
        return (self.z + (k + 8)) % 8

    def y_at(self, k):
        return (self.y + (k + 4)) % 4

    def along_z(self, k):
        return (self.p, self.z_at(k) * 2 + self.c, self.y)

    def along_y(self, k):
        return (self.p, self.d, self.y_at(k))

    def along_x(self, k):
        return ((self.p + (k + 4)) % 4, self.d, self.y)

    def twin(self):
        return (self.p, self.z * 2 + (1 - self.c), self.y)

    def partner(self):
        return (self.p + 1 - 2 * (self.p % 2), self.d, self.y)

    def slab(self, k, y, count=None):
        zz = self.z_at(k)
        at = (zz // 4) * 40 + (zz % 4) * 8 + self.c * 4
        return at + y

    def quad(self, k):
        zz = self.z_at(k)
        return (zz // 4) * 40 + (zz % 4) * 8 + self.c * 4

    def left(self, k):
        zz = self.z_at(k)
        return (zz // 4) * 40 + 32 + (zz % 4) * 2 + self.c


class Gather:
    def __init__(self, here, copies, buf, small, width, cut):
        self.h, self.cp, self.buf, self.small = here, copies, buf, small
        self.width, self.cut = width, cut
        tiles = cut // 128
        self.mid = (tiles + 1) // 2 * 128
        self.c = {}

    def reg_p(self, k, y, part=None):
        lo, hi = {None: (0, self.cut), "a": (0, self.mid), "b": (self.mid, self.cut)}[part]
        return self.buf.at[self.h.slab(k, y), :, pl.ds(lo, hi - lo)]

    def reg_q(self, y, part=None):
        mid = self.cut + (self.width - self.cut + 128) // 256 * 128
        lo, hi = {None: (self.cut, self.width), "a": (self.cut, mid), "b": (mid, self.width)}[part]
        return self.buf.at[self.h.slab(0, y), :, pl.ds(lo, hi - lo)]

    def reg_s(self, y, part=None):
        w = self.width // 4
        mid = w // 256 * 128
        lo, hi = {None: (0, w), "a": (0, mid), "b": (mid, w)}[part]
        return self.small.at[y, :, pl.ds(lo, hi - lo)]

    def reg_quad(self, k, part=None):
        lo, n = {None: (0, 4), "a": (0, 2), "b": (2, 2)}[part]
        return self.buf.at[pl.ds(self.h.quad(k) + lo, n), :, pl.ds(self.cut, self.width - self.cut)]

    def reg_left(self, k, part=None):
        half = self.width // 2
        lo, n = {None: (0, self.width), "a": (0, half), "b": (half, half)}[part]
        return self.buf.at[self.h.left(k), :, pl.ds(lo, n)]

    def go(self, name, region, to):
        self.c[name] = self.cp.start(region, region, to)

    def got(self, name):
        self.c[name].wait_recv()

    def p_send_y(self, k):
        h = self.h
        self.go(("py+", k), self.reg_p(k, h.y), h.along_y(1))
        self.go(("py-", k), self.reg_p(k, h.y), h.along_y(-1))

    def p_forward_y(self, k):
        h = self.h
        self.got(("py+", k))
        self.go(("pyy+", k), self.reg_p(k, h.y_at(-1), "a"), h.along_y(1))
        self.got(("py-", k))
        self.go(("pyy-", k), self.reg_p(k, h.y_at(1), "b"), h.along_y(-1))

    def p_end_y(self, k):
        self.got(("pyy+", k))
        self.got(("pyy-", k))

    def p_send_z(self, k):
        h = self.h
        a, b = (None, None) if k < 3 else ("a", "b")
        self.go(("pz+", k), self.reg_p(-k, h.y, a), h.along_z(1))
        self.go(("pz-", k), self.reg_p(k, h.y, b), h.along_z(-1))

    def q_send_y(self):
        h = self.h
        for tag, reg in (("s", self.reg_s), ("q", self.reg_q)):
            self.go((tag, "y+"), reg(h.y), h.along_y(1))
            self.go((tag, "y-"), reg(h.y), h.along_y(-1))

    def q_forward_y(self):
        h = self.h
        for tag, reg in (("s", self.reg_s), ("q", self.reg_q)):
            self.got((tag, "y+"))
            self.go((tag, "yy+"), reg(h.y_at(-1), "a"), h.along_y(1))
            self.got((tag, "y-"))
            self.go((tag, "yy-"), reg(h.y_at(1), "b"), h.along_y(-1))

    def q_end_y(self):
        self.got(("q", "yy+"))
        self.got(("q", "yy-"))
        self.q_send_z(0, "quad")
        self.got(("s", "yy+"))
        self.got(("s", "yy-"))
        w = self.width // 4
        parts = self.small[...].astype(F32)
        own = self.h.left(0)
        for j in range(4):
            rows = jnp.concatenate([parts[i, 4 * j : 4 * j + 4, :] for i in range(4)], axis=0)
            self.buf[own, :, j * w : (j + 1) * w] = rows.astype(BF)
        self.q_send_z(0, "left")

    def q_send_z(self, k, what):
        h = self.h
        reg = self.reg_quad if what == "quad" else self.reg_left
        a, b = (None, None) if k < 3 else ("a", "b")
        self.go((what, "z+", k), reg(-k, a), h.along_z(1))
        self.go((what, "z-", k), reg(k, b), h.along_z(-1))

    def q_forward_z(self, k):
        for what in ("quad", "left"):
            self.got((what, "z+", k))
            self.got((what, "z-", k))
            if k < 3:
                self.q_send_z(k + 1, what)

    def to_twin(self, k):
        h = self.h
        reg = self.buf.at[pl.ds(h.quad(k), 4)]
        self.go(("t", k), reg, h.twin())
        reg = self.buf.at[h.left(k)]
        self.go(("tl", k), reg, h.twin())

    def round(self, r):
        if r == 0:
            self.q_send_y()
            self.p_send_z(0)
            self.p_send_y(0)
        if r == 1:
            self.q_forward_y()
            self.got(("pz+", 0))
            self.got(("pz-", 0))
            self.p_send_z(1)
            self.p_forward_y(0)
            self.p_send_y(-1)
            self.p_send_y(1)
        if r == 2:
            self.q_end_y()
            self.got(("pz+", 1))
            self.got(("pz-", 1))
            self.p_send_z(2)
            self.p_forward_y(-1)
            self.p_forward_y(1)
            self.p_send_y(-2)
            self.p_send_y(2)
        if r == 3:
            self.got(("pz+", 2))
            self.got(("pz-", 2))
            self.p_send_z(3)
            self.q_forward_z(0)
            self.p_end_y(0)
            self.to_twin(0)
            self.p_forward_y(-2)
            self.p_forward_y(2)
            self.p_send_y(-3)
            self.p_send_y(3)
        if r == 4:
            self.got(("pz+", 3))
            self.got(("pz-", 3))
            self.p_send_y(4)
            self.q_forward_z(1)
            self.p_end_y(-1)
            self.p_end_y(1)
            self.to_twin(-1)
            self.to_twin(1)
            self.p_forward_y(-3)
            self.p_forward_y(3)
        if r == 5:
            self.q_forward_z(2)
            self.p_end_y(-2)
            self.p_end_y(2)
            self.to_twin(-2)
            self.to_twin(2)
            self.p_forward_y(4)
        if r == 6:
            self.p_end_y(-3)
            self.p_end_y(3)
            self.to_twin(-3)
            self.to_twin(3)
            self.p_end_y(4)
            self.q_forward_z(3)
            self.to_twin(4)
        if r == 7:
            for k in (0, -1, 1, -2, 2, -3, 3, 4):
                self.got(("t", k))
                self.got(("tl", k))


def flat(slabs):
    return slabs.reshape(slabs.shape[0] * slabs.shape[1], slabs.shape[2])


def dot(a, b):
    return jnp.dot(a, b, preferred_element_type=F32)


def kernel(
    audio_ref, vision_ref, ids_a_ref, ids_v_ref, order_ref, text_ref, gain_ref, qkv_ref, out_w_ref, proj_ref,
    result_ref,
    w, wp, small, small_p, send_main, send_left, raw_gains, gains,
    x_nat, x_half, xp, bias, perm, normed, packed, macc, mixed, enc, place, prj, text, out_buf,
    send_sem, recv_sem, local_sem,
):
    here = Place()
    h = here.p % 2
    side = here.p // 2
    copies = Copies(send_sem, recv_sem)

    barrier = pltpu.get_barrier_semaphore()
    greet = [here.along_z(1), here.along_z(-1), here.along_y(1), here.along_y(-1), here.along_x(1), here.along_x(-1), here.twin()]
    for to in greet:
        pl.semaphore_signal(barrier, inc=1, device_id=to, device_id_type=MESH)

    @pl.when(side == 0)
    def _():
        pltpu.make_async_copy(audio_ref, x_nat, local_sem.at[0]).start()

    @pl.when(side == 1)
    def _():
        pltpu.make_async_copy(vision_ref, x_nat, local_sem.at[0]).start()

    text_copy = pltpu.make_async_copy(text_ref, text, local_sem.at[1])
    text_copy.start()

    own = here.slab(0, here.y)
    pieces = [(qkv_ref, 0), (qkv_ref, 1280), (qkv_ref, 2560), (out_w_ref, 0)]

    def main_of(i, half):
        ref, base = pieces[i]
        at = pl.multiple_of(base + half * HALF, 128)
        return ref[0, pl.ds(0, 16), pl.ds(at, HALF)]

    def left_of(half):
        rows = []
        for ref, base in pieces:
            at = pl.multiple_of(base + half * HALF, 128)
            rows.append(ref[0, pl.ds(16, 4), pl.ds(at, HALF)].astype(F32))
        return jnp.concatenate(rows, axis=0).astype(BF)

    for i in range(4):
        send_main[:, i * HALF : (i + 1) * HALF] = main_of(i, 1 - h)
    send_left[...] = left_of(1 - h)
    raw_gains[h] = jnp.broadcast_to(gain_ref[...], (16, 1280))

    pl.semaphore_wait(barrier, len(greet))
    x_main = copies.start(send_main, w.at[h, own], here.partner())
    x_left = copies.start(send_left, small.at[h, here.y], here.partner())
    x_gain = copies.start(raw_gains.at[h], raw_gains.at[h], here.partner())

    wp[own] = proj_ref[pl.ds(0, 16), :]
    tail = proj_ref[pl.ds(16, 4), :].astype(F32)
    small_p[here.y] = jnp.concatenate([tail[:, j * 512 : (j + 1) * 512] for j in range(4)], axis=0).astype(BF)
    for i in range(4):
        w[h, own, :, i * HALF : (i + 1) * HALF] = main_of(i, h)
    small[h, here.y] = left_of(h)

    g0 = Gather(here, copies, w.at[0], small.at[0], 2560, 1920)
    g1 = Gather(here, copies, w.at[1], small.at[1], 2560, 1920)
    gp = Gather(here, copies, wp, small_p, 2048, 1536)

    x_main.wait_recv()
    x_left.wait_recv()
    x_gain.wait_recv()
    g0.round(0)

    t = lax.broadcasted_iota(jnp.int32, (1, HALF), 1)
    u = t - 512
    source = jnp.where(t < 512, (t // 16) * 20 + t % 16, (u // 4) * 20 + 16 + u % 4)
    perm[...] = (lax.broadcasted_iota(jnp.int32, (HALF, HALF), 0) == source).astype(F32).astype(BF)

    g0.round(1)
    for b in range(2):
        sl = slice(b * HALF, (b + 1) * HALF)
        for l in range(2):
            gains[l, :, sl] = dot(raw_gains[l, :, sl], perm[...]).astype(BF)

    ids = jnp.where(side == 0, ids_a_ref[...], ids_v_ref[...])
    hot = (lax.broadcasted_iota(jnp.int32, (16, ROWS), 0) == ids).astype(F32).astype(BF)
    same = lax.dot_general(hot, hot, (((0,), (0,)), ((), ())), preferred_element_type=F32)
    bias[...] = (same - 1.0) * 1e30

    @pl.when(side == 0)
    def _():
        pltpu.make_async_copy(audio_ref, x_nat, local_sem.at[0]).wait()

    @pl.when(side == 1)
    def _():
        pltpu.make_async_copy(vision_ref, x_nat, local_sem.at[0]).wait()

    g0.round(2)
    x_half[...] = x_nat[:, pl.ds(pl.multiple_of(h * HALF, 128), HALF)]
    for b in range(2):
        sl = slice(b * HALF, (b + 1) * HALF)
        xp[b] = dot(x_nat[:, sl], perm[...]).astype(BF)
    place[...] = (lax.broadcasted_iota(jnp.int32, (768, 512), 0) == order_ref[:, :512]).astype(F32).astype(BF)

    def norm(l):
        def body(i, carry):
            at = pl.ds(pl.multiple_of(i * 32, 32), 32)
            a = xp[0, at, :].astype(F32)
            b = xp[1, at, :].astype(F32)
            mean = (jnp.sum(a, axis=-1, keepdims=True) + jnp.sum(b, axis=-1, keepdims=True)) * (1.0 / 1280)
            a = a - mean
            b = b - mean
            var = (jnp.sum(a * a, axis=-1, keepdims=True) + jnp.sum(b * b, axis=-1, keepdims=True)) * (1.0 / 1280)
            scale = lax.rsqrt(var + 1e-05)
            gain = gains[l, pl.ds(0, 16), :].astype(F32)[0:1]
            normed[at, pl.ds(0, HALF)] = (a * scale * gain[:, :HALF]).astype(BF)
            normed[at, pl.ds(HALF, HALF)] = (b * scale * gain[:, HALF:]).astype(BF)
            return carry

        lax.fori_loop(0, ROWS // 32, body, 0)

    def project(l, i):
        sl = slice(i * HALF, (i + 1) * HALF)
        packed[:, sl] = dot(normed[...], flat(w[l, :, :, sl])).astype(BF)

    def head(q, k, v, keep, scale):
        s = lax.dot_general(q, jnp.where(keep, k, 0), (((1,), (1,)), ((), ())), preferred_element_type=F32)
        s = s * scale + bias[...]
        e = jnp.exp(s - jnp.max(s, axis=-1, keepdims=True))
        weights = (e / jnp.sum(e, axis=-1, keepdims=True)).astype(BF)
        return dot(weights, jnp.where(keep, v, 0))

    def attend():
        @pl.when(side == 0)
        def _():
            def body(j, carry):
                q, k, v = [packed[:, pl.ds(pl.multiple_of(i * HALF + j * 128, 128), 128)] for i in range(3)]
                lane = lax.broadcasted_iota(jnp.int32, (ROWS, 128), 1)
                total = head(q, k, v, lane < 64, 0.125) + head(q, k, v, lane >= 64, 0.125)
                macc[:, pl.ds(pl.multiple_of(j * 128, 128), 128)] = total
                return carry

            lax.fori_loop(0, 5, body, 0)

        @pl.when(side == 1)
        def _():
            macc[...] = jnp.zeros((ROWS, HALF), F32)
            for i in range(8):
                lo, hi = (80 * i) // 128 * 128, (80 * i + 80 + 127) // 128 * 128
                q, k, v = [packed[:, j * HALF + lo : j * HALF + hi] for j in range(3)]
                lane = lax.broadcasted_iota(jnp.int32, (ROWS, hi - lo), 1) + lo
                keep = (lane >= 80 * i) & (lane < 80 * i + 80)
                macc[:, lo:hi] = macc[:, lo:hi] + head(q, k, v, keep, 80 ** (-0.5))

    def out_layer(l):
        update = dot(mixed[0], flat(w[l, pl.ds(0, 40), :, pl.ds(3 * HALF, HALF)]))
        update = update + dot(mixed[1], flat(w[l, pl.ds(40, 40), :, pl.ds(3 * HALF, HALF)]))
        x_half[...] = (x_half[...].astype(F32) + update).astype(BF)

    g0.round(3)
    g1.round(0)
    g0.round(4)
    g1.round(1)
    g0.round(5)
    norm(0)
    g1.round(2)
    g0.round(6)
    g1.round(3)
    gp.round(0)
    g0.round(7)

    for i in range(3):
        project(0, i)
    g1.round(4)
    gp.round(1)
    attend()
    mixed[h] = dot(macc[...].astype(BF), perm[...]).astype(BF)
    cm0 = copies.start(mixed.at[h], mixed.at[h], here.partner())
    g1.round(5)
    gp.round(2)
    copies.wait(cm0)
    out_layer(0)
    xp[h] = dot(x_half[...], perm[...]).astype(BF)
    cx0 = copies.start(xp.at[h], xp.at[h], here.partner())
    g1.round(6)
    gp.round(3)
    g1.round(7)
    copies.wait(cx0)
    norm(1)
    for i in range(3):
        project(1, i)
    gp.round(4)
    attend()
    mixed[h] = dot(macc[...].astype(BF), perm[...]).astype(BF)
    cm1 = copies.start(mixed.at[h], mixed.at[h], here.partner())
    gp.round(5)
    copies.wait(cm1)
    out_layer(1)
    enc[here.p] = dot(x_half[...], perm[...]).astype(BF)
    up = copies.start(enc.at[here.p], enc.at[here.p], here.along_x(1))
    down = copies.start(enc.at[here.p], enc.at[here.p], here.along_x(-1))
    gp.round(6)
    up.wait_recv()
    lo = enc.at[(here.p + 3) % 4, pl.ds(0, 128)]
    up2 = copies.start(lo, lo, here.along_x(1))
    down.wait_recv()
    hi = enc.at[(here.p + 1) % 4, pl.ds(128, 128)]
    down2 = copies.start(hi, hi, here.along_x(-1))
    gp.round(7)
    text_copy.wait()
    up2.wait_recv()
    down2.wait_recv()

    def last(j, carry):
        cols = pl.ds(pl.multiple_of(j * 512, 512), 512)
        top = flat(wp[pl.ds(0, 40), :, cols])
        low = flat(wp[pl.ds(40, 40), :, cols])
        for i in range(2):
            rows = dot(enc[2 * i], top) + dot(enc[2 * i + 1], low)
            prj[pl.ds(i * ROWS, ROWS), cols] = rows.astype(BF)
        spread = dot(place[...], prj[:, cols])
        taken = jnp.sum(place[...].astype(F32), axis=-1, keepdims=True)
        out_buf[:, cols] = jnp.where(taken > 0.5, spread, text[:, cols].astype(F32)).astype(BF)
        pltpu.make_async_copy(out_buf.at[:, cols], result_ref.at[:, cols], local_sem.at[2 + j]).start()
        return carry

    lax.fori_loop(0, 4, last, 0)
    copies.finish()
    for j in range(4):
        cols = pl.ds(j * 512, 512)
        pltpu.make_async_copy(out_buf.at[:, cols], result_ref.at[:, cols], local_sem.at[2 + j]).wait()


def per_device(audio, vision, ids_a, ids_v, order, text, gain, qkv, out_w, proj):
    vm = pl.BlockSpec(memory_space=pltpu.VMEM)
    anywhere = pl.BlockSpec(memory_space=pl.ANY)
    return pl.pallas_call(
        kernel,
        out_shape=jax.ShapeDtypeStruct((768, 2048), BF),
        in_specs=[anywhere, anywhere, vm, vm, vm, anywhere, vm, vm, vm, vm],
        out_specs=anywhere,
        scratch_shapes=[
            pltpu.VMEM((2, 80, 16, 2560), BF),
            pltpu.VMEM((80, 16, 2048), BF),
            pltpu.VMEM((2, 4, 16, 640), BF),
            pltpu.VMEM((4, 16, 512), BF),
            pltpu.VMEM((16, 2560), BF),
            pltpu.VMEM((16, 640), BF),
            pltpu.VMEM((2, 16, 1280), BF),
            pltpu.VMEM((2, 16, 1280), BF),
            pltpu.VMEM((ROWS, 1280), BF),
            pltpu.VMEM((ROWS, HALF), BF),
            pltpu.VMEM((2, ROWS, HALF), BF),
            pltpu.VMEM((ROWS, ROWS), F32),
            pltpu.VMEM((HALF, HALF), BF),
            pltpu.VMEM((ROWS, 1280), BF),
            pltpu.VMEM((ROWS, 3 * HALF), BF),
            pltpu.VMEM((ROWS, HALF), F32),
            pltpu.VMEM((2, ROWS, HALF), BF),
            pltpu.VMEM((4, ROWS, HALF), BF),
            pltpu.VMEM((768, 512), BF),
            pltpu.VMEM((512, 2048), BF),
            pltpu.VMEM((768, 2048), BF),
            pltpu.VMEM((768, 2048), BF),
            pltpu.SemaphoreType.DMA((N_COPIES,)),
            pltpu.SemaphoreType.DMA((N_COPIES,)),
            pltpu.SemaphoreType.DMA((8,)),
        ],
        name="encode",
        compiler_params=pltpu.CompilerParams(collective_id=0, has_side_effects=True, vmem_limit_bytes=56 * 2**20),
        cost_estimate=pl.CostEstimate(flops=12_000_000_000, bytes_accessed=30_000_000, transcendentals=2_000_000),
    )(audio, vision, ids_a, ids_v, order, text, gain, qkv, out_w, proj)


def solution(mesh):
    placed = (
        P(("dp", "fsdp"), None),
        P(("dp", "fsdp"), None),
        P(("dp", "fsdp"), None),
        P(("dp", "fsdp"), None),
        P(("dp", "fsdp"), None),
        P(("dp", "fsdp"), "phase"),
        P("phase", None),
        P("phase", ("dp", "fsdp"), None),
        P("phase", ("dp", "fsdp"), None),
        P(("dp", "fsdp"), "phase"),
    )
    return jax.shard_map(
        per_device,
        mesh=mesh,
        in_specs=placed,
        out_specs=P(("dp", "fsdp"), "phase"),
        check_vma=False,
    )
```

time: 355 us -> 117 us (0.33)
  waiting for transfers between devices: 269 us -> 0 us
  Pallas kernels: 0 us -> 113 us
  local copies, waits for them, and re-layouts: 45.6 us -> 3.97 us
  matrix products: 21.5 us -> 0 us
  between operations: 13.3 us -> 0.01 us
    all_gather x3 -> x0, waiting for transfers between devices: 209 us -> none  [the longest x1 101 us: per_device(): lax.all_gather(attn_qkv[0], ('dp', 'fsdp'), axis=0, tiled=True)]
    pallas_call x0 -> x1, Pallas kernels: none -> 113 us  [per_device(): pl.pallas_call(kernel, out_shape=jax.ShapeDtypeStruct((768, 2048), BF), i...]
    psum x1 -> x0, waiting for transfers between devices: 42.3 us -> none  [broadcast(): return lax.psum(kept, axis)]
    unnamed x22 -> x1, local copies, waits for them, and re-layouts: 34.1 us -> 3.97 us
    dot_general x4 -> x0, matrix products: 18.1 us -> none  [the longest x1 6.63 us: full_layer(): jnp.dot(normed, own_qkv, preferred_element_type=jnp.float32)]
    ppermute x1 -> x0, waiting for transfers between devices: 16.9 us -> none  [shifted(): return lax.ppermute(shard, axis, pairs)]
    scatter x1 -> x0, local copies, waits for them, and re-layouts: 7.57 us -> none  [per_device(): return text_embeds.at[insert_order[0, :2 * row_count]].set(projected)]
  transfers between devices with their start and end apart: 5 -> 0, of which waited for: 5 -> 0; matrix products, arithmetic and copies ran while one was open for 14% -> 0% of each run, Pallas kernels for 0% -> 0%
where the time goes in v1:
time: 117 us
  Pallas kernels  113 us (97%)
  local copies, waits for them, and re-layouts  3.97 us (3%)
    pallas_call x1, Pallas kernels, per_device(): pl.pallas_call(kernel, out_shape=jax.ShapeDtypeStruct((768, 2048), BF), i...  113 us
    unnamed x1, local copies, waits for them, and re-layouts  3.97 us

profile of v1, /device:TPU:4, one launch (start us, length us, event | category | flops | bytes accessed | tf_op | source)
XLA Modules:
  0.0 117.2 jit_solution(478336391768626431)
XLA Ops:
  0.0 113.2 %encode.1 = bf16[768,2048]{1,0:T(8,128)(2,1)} custom-call(bf16[256,1280]{1,0:T(8,128)(2,1)} %audio_ref.1, bf16[256,1280]{1,0:T(8,128)(2,1)} %vision_ref.1, s32[1,256]{1,0:T(1,128)} %ids_a_ref.1, s32[1,256]{1,0:T(1,128)} %ids_v_ref.1, s32[1,768]{1,0:T(1,128)} %order_ref.1, bf16[768,2048]{1,0:T(8,128)(2,1)} %text_ref.1, bf16[1,1280]{1,0:T(2,128)(2,1)} %gain_ref.1, ...), custom_call_target="tpu_custom_call" | custom-call | flops 12000000000 | bytes 30000000 | tf_op jit(solution)/shard_map/encode/pallas_call | solution.py:501
  113.3 4.0 %copy.12 = bf16[768,2048]{1,0:T(8,128)(2,1)} copy(bf16[768,2048]{1,0:T(8,128)(2,1)} %encode.1) | data formatting | bytes 6291456

commit v2 on v1

v2 whole, which is shorter than its diff:
```python
import jax
import jax.numpy as jnp
from jax import lax
from jax.experimental import pallas as pl
from jax.experimental.pallas import tpu as pltpu
from jax.sharding import PartitionSpec as P

MESH = pl.DeviceIdType.MESH
BF = jnp.bfloat16
F32 = jnp.float32
ROWS = 256
HALF = 640
N_SEND = 52
N_RECV = 180
CHUNK = 128


class Copies:
    def __init__(self, send, recv):
        self.send, self.recv = send, recv
        self.at, self.groups, self.sent = [0, 0], {}, []

    def sem(self, kind, name):
        if (kind, name) not in self.groups:
            self.groups[kind, name] = self.at[kind]
            self.at[kind] += 1
        return (self.send, self.recv)[kind].at[self.groups[kind, name]]

    def start(self, src, dst, to, send=None, recv=None):
        alone = send is None
        if alone:
            send = recv = ("alone", len(self.sent))
        copy = pltpu.make_async_remote_copy(
            src_ref=src,
            dst_ref=dst,
            send_sem=self.sem(0, send),
            recv_sem=self.sem(1, recv),
            device_id=to,
            device_id_type=MESH,
        )
        copy.start()
        if alone:
            self.sent.append(copy)
        return copy

    def wait(self, kind, name, size, to):
        copy = pltpu.make_async_remote_copy(
            src_ref=size,
            dst_ref=size,
            send_sem=self.sem(0, name) if kind == 0 else self.send.at[0],
            recv_sem=self.sem(1, name) if kind == 1 else self.recv.at[0],
            device_id=to,
            device_id_type=MESH,
        )
        if kind == 0:
            copy.wait_send()
        else:
            copy.wait_recv()

    def finish(self):
        for copy in self.sent:
            copy.wait_send()


class Place:
    def __init__(self):
        self.p = lax.axis_index("phase")
        self.d = lax.axis_index("dp")
        self.y = lax.axis_index("fsdp")
        self.z = self.d // 2
        self.c = self.d % 2

    def z_at(self, k):
        return (self.z + (k + 8)) % 8

    def y_at(self, k):
        return (self.y + (k + 4)) % 4

    def along_z(self, k):
        return (self.p, self.z_at(k) * 2 + self.c, self.y)

    def along_y(self, k):
        return (self.p, self.d, self.y_at(k))

    def along_x(self, k):
        return ((self.p + (k + 4)) % 4, self.d, self.y)

    def twin(self):
        return (self.p, self.z * 2 + (1 - self.c), self.y)

    def partner(self):
        return self.along_x(1 - 2 * (self.p % 2))

    def across(self):
        return self.along_x(2 * (self.p % 2) - 1)

    def slab(self, k, y, count=None):
        zz = self.z_at(k)
        at = (zz // 4) * 40 + (zz % 4) * 8 + self.c * 4
        return at + y

    def quad(self, k):
        zz = self.z_at(k)
        return (zz // 4) * 40 + (zz % 4) * 8 + self.c * 4

    def left(self, k):
        zz = self.z_at(k)
        return (zz // 4) * 40 + 32 + (zz % 4) * 2 + self.c


class Gather:
    def __init__(self, tag, here, copies, buf, small, cut):
        self.tag = tag
        self.h, self.cp, self.buf, self.small = here, copies, buf, small
        self.width, self.cut = buf.shape[2], cut
        self.short = small.shape[2]
        tiles = cut // 128
        self.mid = (tiles + 1) // 2 * 128

    def reg_p(self, k, y, part=None):
        lo, hi = {None: (0, self.cut), "a": (0, self.mid), "b": (self.mid, self.cut)}[part]
        return self.buf.at[self.h.slab(k, y), :, pl.ds(lo, hi - lo)]

    def reg_q(self, y, part=None):
        mid = self.cut + (self.width - self.cut + 128) // 256 * 128
        lo, hi = {None: (self.cut, self.width), "a": (self.cut, mid), "b": (mid, self.width)}[part]
        return self.buf.at[self.h.slab(0, y), :, pl.ds(lo, hi - lo)]

    def reg_s(self, y, part=None):
        w = self.short
        mid = w // 256 * 128
        lo, hi = {None: (0, w), "a": (0, mid), "b": (mid, w)}[part]
        return self.small.at[y, :, pl.ds(lo, hi - lo)]

    def reg_quad(self, k, part=None):
        lo, n = {None: (0, 4), "a": (0, 2), "b": (2, 2)}[part]
        return self.buf.at[pl.ds(self.h.quad(k) + lo, n), :, pl.ds(self.cut, self.width - self.cut)]

    def reg_left(self, k, part=None):
        half = self.width // 256 * 128
        lo, n = {None: (0, self.width), "a": (0, half), "b": (half, self.width - half)}[part]
        return self.buf.at[self.h.left(k), :, pl.ds(lo, n)]

    def go(self, kind, group, region, to):
        self.cp.start(region, region, to, (self.tag, kind), (self.tag, kind, group))

    def size(self, kind, n):
        if kind[0] == "p":
            return self.buf.at[pl.ds(0, n), :, pl.ds(0, self.cut)]
        if kind == "quad":
            return self.buf.at[pl.ds(0, 4 * n), :, pl.ds(self.cut, self.width - self.cut)]
        if kind == "q":
            return self.buf.at[pl.ds(0, n), :, pl.ds(self.cut, self.width - self.cut)]
        if kind == "s":
            return self.small.at[pl.ds(0, n)]
        return self.buf.at[pl.ds(0, n)]

    def got(self, kind, group, n):
        self.cp.wait(1, (self.tag, kind, group), self.size(kind, n), self.h.twin())

    def finish(self):
        for kind, n in (("pz", 7), ("py", 24), ("quad", 7), ("left", 7), ("s", 3), ("q", 3), ("t", 40)):
            self.cp.wait(0, (self.tag, kind), self.size(kind, n), self.h.twin())

    def p_send_y(self, k):
        h = self.h
        self.go("py", k, self.reg_p(k, h.y), h.along_y(1))
        self.go("py", k, self.reg_p(k, h.y), h.along_y(-1))

    def p_forward_y(self, k):
        h = self.h
        self.got("py", k, 2)
        self.go("py", ("far", k), self.reg_p(k, h.y_at(-1), "a"), h.along_y(1))
        self.go("py", ("far", k), self.reg_p(k, h.y_at(1), "b"), h.along_y(-1))

    def p_end_y(self, k):
        self.got("py", ("far", k), 1)

    def p_send_z(self, k):
        h = self.h
        a, b = (None, None) if k < 3 else ("a", "b")
        self.go("pz", k, self.reg_p(-k, h.y, a), h.along_z(1))
        self.go("pz", k, self.reg_p(k, h.y, b), h.along_z(-1))

    def p_got_z(self, k):
        self.got("pz", k, 2 if k < 3 else 1)

    def q_send_y(self):
        h = self.h
        for tag, reg in (("s", self.reg_s), ("q", self.reg_q)):
            self.go(tag, 0, reg(h.y), h.along_y(1))
            self.go(tag, 0, reg(h.y), h.along_y(-1))

    def q_forward_y(self):
        h = self.h
        for tag, reg in (("s", self.reg_s), ("q", self.reg_q)):
            self.got(tag, 0, 2)
            self.go(tag, 1, reg(h.y_at(-1), "a"), h.along_y(1))
            self.go(tag, 1, reg(h.y_at(1), "b"), h.along_y(-1))

    def q_end_y(self):
        self.got("q", 1, 1)
        self.q_send_z(0, "quad")
        self.got("s", 1, 1)
        self.gather_left()
        self.q_send_z(0, "left")

    def gather_left(self):
        parts = self.small[...].astype(F32)
        own = self.h.left(0)
        for j in range(4):
            lo, hi = j * self.short, min((j + 1) * self.short, self.width)
            rows = jnp.concatenate([parts[i, 4 * j : 4 * j + 4, : hi - lo] for i in range(4)], axis=0)
            self.buf[own, :, lo:hi] = rows.astype(BF)

    def q_send_z(self, k, what):
        h = self.h
        reg = self.reg_quad if what == "quad" else self.reg_left
        a, b = (None, None) if k < 3 else ("a", "b")
        self.go(what, k, reg(-k, a), h.along_z(1))
        self.go(what, k, reg(k, b), h.along_z(-1))

    def q_forward_z(self, k):
        for what in ("quad", "left"):
            self.got(what, k, 2 if k < 3 else 1)
            if k < 3:
                self.q_send_z(k + 1, what)

    def to_twin(self, k):
        h = self.h
        self.go("t", 0, self.buf.at[pl.ds(h.quad(k), 4)], h.twin())
        self.go("t", 0, self.buf.at[h.left(k)], h.twin())

    def round(self, r):
        if r == 0:
            self.q_send_y()
            self.p_send_z(0)
            self.p_send_y(0)
        if r == 1:
            self.p_got_z(0)
            self.p_send_z(1)
            self.q_forward_y()
            self.p_send_y(-1)
            self.p_send_y(1)
            self.p_forward_y(0)
        if r == 2:
            self.q_end_y()
            self.p_got_z(1)
            self.p_send_z(2)
            self.p_send_y(-2)
            self.p_send_y(2)
            self.p_forward_y(-1)
            self.p_forward_y(1)
        if r == 3:
            self.p_got_z(2)
            self.p_send_z(3)
            self.q_forward_z(0)
            self.p_send_y(-3)
            self.p_send_y(3)
            self.p_forward_y(-2)
            self.p_forward_y(2)
            self.p_end_y(0)
            self.to_twin(0)
        if r == 4:
            self.p_got_z(3)
            self.p_send_y(4)
            self.q_forward_z(1)
            self.p_forward_y(-3)
            self.p_forward_y(3)
            self.p_end_y(-1)
            self.p_end_y(1)
            self.to_twin(-1)
            self.to_twin(1)
        if r == 5:
            self.q_forward_z(2)
            self.p_forward_y(4)
            self.p_end_y(-2)
            self.p_end_y(2)
            self.to_twin(-2)
            self.to_twin(2)
        if r == 6:
            self.q_forward_z(3)
            self.p_end_y(-3)
            self.p_end_y(3)
            self.to_twin(-3)
            self.to_twin(3)
            self.p_end_y(4)
            self.to_twin(4)
        if r == 7:
            self.got("t", 0, 40)


def flat(slabs):
    return slabs.reshape(slabs.shape[0] * slabs.shape[1], slabs.shape[2])


def dot(a, b):
    return jnp.dot(a, b, preferred_element_type=F32)


def compact(rows, short):
    rows = rows.astype(F32)
    fill = 4 * short - rows.shape[1]
    if fill:
        rows = jnp.concatenate([rows, jnp.zeros((4, fill), F32)], axis=1)
    return jnp.concatenate([rows[:, j * short : (j + 1) * short] for j in range(4)], axis=0).astype(BF)


def kernel(
    audio_ref, vision_ref, ids_a_ref, ids_v_ref, order_ref, text_ref, gain_ref, qkv_ref, out_w_ref, proj_ref,
    result_ref,
    wq, wo, wp, small_q, small_o, small_p, send_q, send_sq, raw_gains, gains,
    x_nat, xp, bias, perm, normed, packed, macc, mixed, enc, place, text, out_buf,
    send_sem, recv_sem, local_sem,
):
    here = Place()
    h = here.p % 2
    side = here.p // 2
    copies = Copies(send_sem, recv_sem)

    barrier = pltpu.get_barrier_semaphore()
    greet = [here.along_z(1), here.along_z(-1), here.along_y(1), here.along_y(-1), here.along_x(1), here.along_x(-1), here.twin()]
    for to in greet:
        pl.semaphore_signal(barrier, inc=1, device_id=to, device_id_type=MESH)

    @pl.when(side == 0)
    def _():
        pltpu.make_async_copy(audio_ref, x_nat, local_sem.at[0]).start()

    @pl.when(side == 1)
    def _():
        pltpu.make_async_copy(vision_ref, x_nat, local_sem.at[0]).start()

    text_copy = pltpu.make_async_copy(text_ref, text, local_sem.at[1])
    text_copy.start()

    own = here.slab(0, here.y)

    def part(rows, half, i):
        at = pl.multiple_of(i * 1280 + half * HALF, 128)
        return qkv_ref[0, rows, pl.ds(at, HALF)]

    first, rest = pl.ds(0, 16), pl.ds(16, 4)

    def left_of(half):
        return compact(jnp.concatenate([part(rest, half, i).astype(F32) for i in range(3)], axis=1), 512)

    for i in range(3):
        send_q[:, i * HALF : (i + 1) * HALF] = part(first, 1 - h, i)
    send_sq[...] = left_of(1 - h)
    wo[h, own] = out_w_ref[0, pl.ds(0, 16), :]
    small_o[h, here.y] = compact(out_w_ref[0, pl.ds(16, 4), :], 384)
    raw_gains[h] = jnp.broadcast_to(gain_ref[...], (16, 1280))

    pl.semaphore_wait(barrier, len(greet))
    exchange = [
        copies.start(send_q, wq.at[h, own], here.partner()),
        copies.start(send_sq, small_q.at[h, here.y], here.partner()),
        copies.start(wo.at[h, own], wo.at[h, own], here.partner()),
        copies.start(small_o.at[h, here.y], small_o.at[h, here.y], here.partner()),
        copies.start(raw_gains.at[h], raw_gains.at[h], here.partner()),
    ]

    wp[own] = proj_ref[pl.ds(0, 16), :]
    small_p[here.y] = compact(proj_ref[pl.ds(16, 4), :], 512)
    gp = Gather(0, here, copies, wp, small_p, 1536)
    gp.round(0)
    for i in range(3):
        wq[h, own, :, i * HALF : (i + 1) * HALF] = part(first, h, i)
    small_q[h, here.y] = left_of(h)

    a0 = Gather(1, here, copies, wq.at[0], small_q.at[0], 1408)
    a1 = Gather(2, here, copies, wq.at[1], small_q.at[1], 1408)
    b0 = Gather(3, here, copies, wo.at[0], small_o.at[0], 1024)
    b1 = Gather(4, here, copies, wo.at[1], small_o.at[1], 1024)

    for copy in exchange[:2]:
        copy.wait_recv()
    a0.round(0)
    for copy in exchange[2:]:
        copy.wait_recv()

    def prepare_perm():
        t = lax.broadcasted_iota(jnp.int32, (1, HALF), 1)
        u = t - 512
        source = jnp.where(t < 512, (t // 16) * 20 + t % 16, (u // 4) * 20 + 16 + u % 4)
        perm[...] = (lax.broadcasted_iota(jnp.int32, (HALF, HALF), 0) == source).astype(F32).astype(BF)

    def prepare_rows():
        @pl.when(side == 0)
        def _():
            pltpu.make_async_copy(audio_ref, x_nat, local_sem.at[0]).wait()

        @pl.when(side == 1)
        def _():
            pltpu.make_async_copy(vision_ref, x_nat, local_sem.at[0]).wait()

        for b in range(2):
            sl = slice(b * HALF, (b + 1) * HALF)
            for l in range(2):
                gains[l, :, sl] = dot(raw_gains[l, :, sl], perm[...]).astype(BF)
            xp[b] = dot(x_nat[:, sl], perm[...]).astype(BF)

    def prepare_bias():
        ids = jnp.where(side == 0, ids_a_ref[...], ids_v_ref[...])
        hot = (lax.broadcasted_iota(jnp.int32, (16, ROWS), 0) == ids).astype(F32).astype(BF)
        same = lax.dot_general(hot, hot, (((0,), (0,)), ((), ())), preferred_element_type=F32)
        bias[...] = (same - 1.0) * 1e30

    def prepare_place():
        place[...] = (lax.broadcasted_iota(jnp.int32, (768, 512), 0) == order_ref[:, :512]).astype(F32).astype(BF)

    def prepare_text():
        text_copy.wait()

        def body(i, carry):
            at = pl.ds(pl.multiple_of(i * 64, 64), 64)
            taken = jnp.sum(place[at, :].astype(F32), axis=-1, keepdims=True)
            text[at, :] = jnp.where(taken > 0.5, 0.0, text[at, :].astype(F32)).astype(BF)
            return carry

        lax.fori_loop(0, 12, body, 0)

    def norm(l, c):
        def body(i, carry):
            at = pl.ds(pl.multiple_of(c * CHUNK + i * 32, 32), 32)
            a = xp[0, at, :].astype(F32)
            b = xp[1, at, :].astype(F32)
            mean = (jnp.sum(a, axis=-1, keepdims=True) + jnp.sum(b, axis=-1, keepdims=True)) * (1.0 / 1280)
            a = a - mean
            b = b - mean
            var = (jnp.sum(a * a, axis=-1, keepdims=True) + jnp.sum(b * b, axis=-1, keepdims=True)) * (1.0 / 1280)
            scale = lax.rsqrt(var + 1e-05)
            gain = gains[l, pl.ds(0, 16), :].astype(F32)[0:1]
            normed[at, pl.ds(0, HALF)] = (a * scale * gain[:, :HALF]).astype(BF)
            normed[at, pl.ds(HALF, HALF)] = (b * scale * gain[:, HALF:]).astype(BF)
            return carry

        lax.fori_loop(0, CHUNK // 32, body, 0)

    def project(l):
        for i in range(3):
            sl = slice(i * HALF, (i + 1) * HALF)
            packed[:, sl] = dot(normed[...], flat(wq[l, :, :, sl])).astype(BF)

    def head(q, k, v, mask, keep, scale):
        s = lax.dot_general(q, jnp.where(keep, k, 0), (((1,), (1,)), ((), ())), preferred_element_type=F32)
        s = s * scale + mask
        e = jnp.exp(s - jnp.max(s, axis=-1, keepdims=True))
        weights = (e / jnp.sum(e, axis=-1, keepdims=True)).astype(BF)
        return dot(weights, jnp.where(keep, v, 0))

    def attend(l, c):
        at = pl.ds(c * CHUNK, CHUNK)

        @pl.when(side == 0)
        def _():
            def body(j, carry):
                q, k, v = [
                    packed[at if i == 0 else pl.ds(0, ROWS), pl.ds(pl.multiple_of(i * HALF + j * 128, 128), 128)]
                    for i in range(3)
                ]
                low = lax.broadcasted_iota(jnp.int32, (ROWS, 128), 1) < 64
                mask = bias[at, :]
                total = head(q, k, v, mask, low, 0.125) + head(q, k, v, mask, jnp.logical_not(low), 0.125)
                mixed[l, h, at, pl.ds(pl.multiple_of(j * 128, 128), 128)] = total.astype(BF)
                return carry

            lax.fori_loop(0, 5, body, 0)

        @pl.when(side == 1)
        def _():
            macc[...] = jnp.zeros((CHUNK, HALF), F32)
            for i in range(8):
                lo, hi = (80 * i) // 128 * 128, (80 * i + 80 + 127) // 128 * 128
                q, k, v = [packed[at if j == 0 else pl.ds(0, ROWS), j * HALF + lo : j * HALF + hi] for j in range(3)]
                lane = lax.broadcasted_iota(jnp.int32, (ROWS, hi - lo), 1) + lo
                keep = (lane >= 80 * i) & (lane < 80 * i + 80)
                macc[:, lo:hi] = macc[:, lo:hi] + head(q, k, v, bias[at, :], keep, 80 ** (-0.5))
            mixed[l, h, at, :] = macc[...].astype(BF)

        piece = mixed.at[l, h, at, :]
        return copies.start(piece, piece, here.partner())

    def out_layer(l, c, copy, to):
        copy.wait_recv()
        at = pl.ds(c * CHUNK, CHUNK)
        update = None
        for b in range(2):
            rows = dot(mixed[l, b, at, :], perm[...]).astype(BF)
            term = dot(rows, flat(wo[l, pl.ds(40 * b, 40), :, :]))
            update = term if update is None else update + term
        x_new = (x_nat[at, :].astype(F32) + update).astype(BF)
        x_nat[at, :] = x_new
        for b in range(2):
            to[b, at, :] = dot(x_nat[at, pl.ds(b * HALF, HALF)], perm[...]).astype(BF)

    def columns(j):
        return pl.ds(pl.multiple_of(j * 512, 512), 512)

    def own_rows(j, carry):
        cols = columns(j)
        rows = dot(enc[side, 0], flat(wp[pl.ds(0, 40), :, cols])) + dot(enc[side, 1], flat(wp[pl.ds(40, 40), :, cols]))
        spread = dot(place[:, pl.ds(pl.multiple_of(side * ROWS, ROWS), ROWS)], rows.astype(BF))
        text[:, cols] = (text[:, cols].astype(F32) + spread).astype(BF)
        return carry

    def other_rows(j, carry):
        cols = columns(j)
        o = 1 - side
        rows = dot(enc[o, 0], flat(wp[pl.ds(0, 40), :, cols])) + dot(enc[o, 1], flat(wp[pl.ds(40, 40), :, cols]))
        spread = dot(place[:, pl.ds(pl.multiple_of(o * ROWS, ROWS), ROWS)], rows.astype(BF))
        out_buf[:, cols] = (text[:, cols].astype(F32) + spread).astype(BF)
        pltpu.make_async_copy(out_buf.at[:, cols], result_ref.at[:, cols], local_sem.at[2 + j]).start()
        return carry

    b0.round(0)
    prepare_perm()
    a0.round(1)
    b0.round(1)
    gp.round(1)
    prepare_rows()
    a0.round(2)
    b0.round(2)
    a1.round(0)
    prepare_bias()
    a0.round(3)
    b0.round(3)
    a1.round(1)
    gp.round(2)
    prepare_place()
    a0.round(4)
    b0.round(4)
    a1.round(2)
    norm(0, 0)
    norm(0, 1)
    a0.round(5)
    b0.round(5)
    a1.round(3)
    gp.round(3)
    a0.round(6)
    a1.round(4)
    a0.round(7)
    project(0)
    b0.round(6)
    b1.round(0)
    m0 = attend(0, 0)
    m1 = attend(0, 1)
    b0.round(7)
    a1.round(5)
    b1.round(1)
    out_layer(0, 0, m0, xp)
    norm(1, 0)
    a1.round(6)
    b1.round(2)
    gp.round(4)
    out_layer(0, 1, m1, xp)
    norm(1, 1)
    a1.round(7)
    project(1)
    b1.round(3)
    m0 = attend(1, 0)
    m1 = attend(1, 1)
    b1.round(4)
    gp.round(5)
    b1.round(5)
    gp.round(6)
    prepare_text()
    b1.round(6)
    b1.round(7)

    def send_across(c):
        piece = enc.at[side, h, pl.ds(c * CHUNK, CHUNK), :]
        return copies.start(piece, piece, here.across())

    def pass_on(c, copy):
        copy.wait_recv()
        piece = enc.at[1 - side, 1 - h, pl.ds(c * CHUNK, CHUNK), :]
        return copies.start(piece, piece, here.partner())

    mine = enc.at[side]
    out_layer(1, 0, m0, mine)
    e0 = send_across(0)
    out_layer(1, 1, m1, mine)
    e1 = send_across(1)
    gp.round(7)
    f0 = pass_on(0, e0)
    lax.fori_loop(0, 2, own_rows, 0)
    f1 = pass_on(1, e1)
    lax.fori_loop(2, 4, own_rows, 0)
    f0.wait_recv()
    f1.wait_recv()
    lax.fori_loop(0, 4, other_rows, 0)
    copies.finish()
    for gather in (a0, b0, a1, b1, gp):
        gather.finish()
    assert copies.at[0] <= N_SEND and copies.at[1] <= N_RECV
    for j in range(4):
        cols = pl.ds(j * 512, 512)
        pltpu.make_async_copy(out_buf.at[:, cols], result_ref.at[:, cols], local_sem.at[2 + j]).wait()


def per_device(audio, vision, ids_a, ids_v, order, text, gain, qkv, out_w, proj):
    vm = pl.BlockSpec(memory_space=pltpu.VMEM)
    anywhere = pl.BlockSpec(memory_space=pl.ANY)
    return pl.pallas_call(
        kernel,
        out_shape=jax.ShapeDtypeStruct((768, 2048), BF),
        in_specs=[anywhere, anywhere, vm, vm, vm, anywhere, vm, vm, vm, vm],
        out_specs=anywhere,
        scratch_shapes=[
            pltpu.VMEM((2, 80, 16, 1920), BF),
            pltpu.VMEM((2, 80, 16, 1280), BF),
            pltpu.VMEM((80, 16, 2048), BF),
            pltpu.VMEM((2, 4, 16, 512), BF),
            pltpu.VMEM((2, 4, 16, 384), BF),
            pltpu.VMEM((4, 16, 512), BF),
            pltpu.VMEM((16, 1920), BF),
            pltpu.VMEM((16, 512), BF),
            pltpu.VMEM((2, 16, 1280), BF),
            pltpu.VMEM((2, 16, 1280), BF),
            pltpu.VMEM((ROWS, 1280), BF),
            pltpu.VMEM((2, ROWS, HALF), BF),
            pltpu.VMEM((ROWS, ROWS), F32),
            pltpu.VMEM((HALF, HALF), BF),
            pltpu.VMEM((ROWS, 1280), BF),
            pltpu.VMEM((ROWS, 3 * HALF), BF),
            pltpu.VMEM((CHUNK, HALF), F32),
            pltpu.VMEM((2, 2, ROWS, HALF), BF),
            pltpu.VMEM((2, 2, ROWS, HALF), BF),
            pltpu.VMEM((768, 512), BF),
            pltpu.VMEM((768, 2048), BF),
            pltpu.VMEM((768, 2048), BF),
            pltpu.SemaphoreType.DMA((N_SEND,)),
            pltpu.SemaphoreType.DMA((N_RECV,)),
            pltpu.SemaphoreType.DMA((8,)),
        ],
        name="encode",
        compiler_params=pltpu.CompilerParams(collective_id=0, has_side_effects=True, vmem_limit_bytes=56 * 2**20),
        cost_estimate=pl.CostEstimate(flops=12_000_000_000, bytes_accessed=30_000_000, transcendentals=2_000_000),
    )(audio, vision, ids_a, ids_v, order, text, gain, qkv, out_w, proj)


def solution(mesh):
    placed = (
        P(("dp", "fsdp"), None),
        P(("dp", "fsdp"), None),
        P(("dp", "fsdp"), None),
        P(("dp", "fsdp"), None),
        P(("dp", "fsdp"), None),
        P(("dp", "fsdp"), "phase"),
        P("phase", None),
        P("phase", ("dp", "fsdp"), None),
        P("phase", ("dp", "fsdp"), None),
        P(("dp", "fsdp"), "phase"),
    )
    return jax.shard_map(
        per_device,
        mesh=mesh,
        in_specs=placed,
        out_specs=P(("dp", "fsdp"), "phase"),
        check_vma=False,
    )
```

time: 117 us -> 112 us (0.957)
  Pallas kernels: 113 us -> 108 us
    pallas_call x1, Pallas kernels: 113 us -> 108 us  [per_device(): pl.pallas_call(kernel, out_shape=jax.ShapeDtypeStruct((768, 2048), BF), i...]
where the time goes in v2:
time: 112 us
  Pallas kernels  108 us (96%)
  local copies, waits for them, and re-layouts  3.97 us (4%)
    pallas_call x1, Pallas kernels, per_device(): pl.pallas_call(kernel, out_shape=jax.ShapeDtypeStruct((768, 2048), BF), i...  108 us
    unnamed x1, local copies, waits for them, and re-layouts  3.97 us

profile of v2, /device:TPU:4, one launch (start us, length us, event | category | flops | bytes accessed | tf_op | source)
XLA Modules:
  0.0 111.9 jit_solution(10802202315913060464)
XLA Ops:
  0.0 108.0 %encode.1 = bf16[768,2048]{1,0:T(8,128)(2,1)} custom-call(bf16[256,1280]{1,0:T(8,128)(2,1)} %audio_ref.1, bf16[256,1280]{1,0:T(8,128)(2,1)} %vision_ref.1, s32[1,256]{1,0:T(1,128)} %ids_a_ref.1, s32[1,256]{1,0:T(1,128)} %ids_v_ref.1, s32[1,768]{1,0:T(1,128)} %order_ref.1, bf16[768,2048]{1,0:T(8,128)(2,1)} %text_ref.1, bf16[1,1280]{1,0:T(2,128)(2,1)} %gain_ref.1, ...), custom_call_target="tpu_custom_call" | custom-call | flops 12000000000 | bytes 30000000 | tf_op jit(solution)/shard_map/encode/pallas_call | solution.py:606
  108.0 4.0 %copy.12 = bf16[768,2048]{1,0:T(8,128)(2,1)} copy(bf16[768,2048]{1,0:T(8,128)(2,1)} %encode.1) | data formatting | bytes 6291456

commit v3 on v2

--- a/solution.py
+++ b/solution.py
@@ -11,7 +11,7 @@
 ROWS = 256
 HALF = 640
 N_SEND = 52
-N_RECV = 180
+N_RECV = 182
 CHUNK = 128
 
 
@@ -570,26 +570,28 @@
     b1.round(7)
 
     def send_across(c):
-        piece = enc.at[side, h, pl.ds(c * CHUNK, CHUNK), :]
+        piece = enc.at[side, h, pl.ds(c * 64, 64), :]
         return copies.start(piece, piece, here.across())
 
     def pass_on(c, copy):
         copy.wait_recv()
-        piece = enc.at[1 - side, 1 - h, pl.ds(c * CHUNK, CHUNK), :]
+        piece = enc.at[1 - side, 1 - h, pl.ds(c * 64, 64), :]
         return copies.start(piece, piece, here.partner())
 
     mine = enc.at[side]
     out_layer(1, 0, m0, mine)
-    e0 = send_across(0)
+    e0 = [send_across(0), send_across(1)]
     out_layer(1, 1, m1, mine)
-    e1 = send_across(1)
+    e1 = [send_across(2), send_across(3)]
     gp.round(7)
-    f0 = pass_on(0, e0)
-    lax.fori_loop(0, 2, own_rows, 0)
-    f1 = pass_on(1, e1)
+    f0 = [pass_on(0, e0[0]), pass_on(1, e0[1])]
+    lax.fori_loop(0, 1, own_rows, 0)
+    f1 = [pass_on(2, e1[0])]
+    lax.fori_loop(1, 2, own_rows, 0)
+    f1.append(pass_on(3, e1[1]))
     lax.fori_loop(2, 4, own_rows, 0)
-    f0.wait_recv()
-    f1.wait_recv()
+    for copy in f0 + f1:
+        copy.wait_recv()
     lax.fori_loop(0, 4, other_rows, 0)
     copies.finish()
     for gather in (a0, b0, a1, b1, gp):

time: 112 us -> 111 us (level)
  Pallas kernels: 108 us -> 106 us
    pallas_call x1, Pallas kernels: 108 us -> 106 us  [per_device(): pl.pallas_call(kernel, out_shape=jax.ShapeDtypeStruct((768, 2048), BF), i...]
where the time goes in v3:
time: 111 us; the launch traced here: 110 us
  Pallas kernels  106 us (95%)
  local copies, waits for them, and re-layouts  3.97 us (4%)
    pallas_call x1, Pallas kernels, per_device(): pl.pallas_call(kernel, out_shape=jax.ShapeDtypeStruct((768, 2048), BF), i...  106 us
    unnamed x1, local copies, waits for them, and re-layouts  3.97 us

profile of v3, /device:TPU:4, one launch (start us, length us, event | category | flops | bytes accessed | tf_op | source)
XLA Modules:
  0.0 110.2 jit_solution(3295643240754114496)
XLA Ops:
  0.0 106.2 %encode.1 = bf16[768,2048]{1,0:T(8,128)(2,1)} custom-call(bf16[256,1280]{1,0:T(8,128)(2,1)} %audio_ref.1, bf16[256,1280]{1,0:T(8,128)(2,1)} %vision_ref.1, s32[1,256]{1,0:T(1,128)} %ids_a_ref.1, s32[1,256]{1,0:T(1,128)} %ids_v_ref.1, s32[1,768]{1,0:T(1,128)} %order_ref.1, bf16[768,2048]{1,0:T(8,128)(2,1)} %text_ref.1, bf16[1,1280]{1,0:T(2,128)(2,1)} %gain_ref.1, ...), custom_call_target="tpu_custom_call" | custom-call | flops 12000000000 | bytes 30000000 | tf_op jit(solution)/shard_map/encode/pallas_call | solution.py:608
  106.2 4.0 %copy.12 = bf16[768,2048]{1,0:T(8,128)(2,1)} copy(bf16[768,2048]{1,0:T(8,128)(2,1)} %encode.1) | data formatting | bytes 6291456

commit v4 on v3

--- a/solution.py
+++ b/solution.py
@@ -447,7 +447,7 @@
         s = lax.dot_general(q, jnp.where(keep, k, 0), (((1,), (1,)), ((), ())), preferred_element_type=F32)
         s = s * scale + mask
         e = jnp.exp(s - jnp.max(s, axis=-1, keepdims=True))
-        weights = (e / jnp.sum(e, axis=-1, keepdims=True)).astype(BF)
+        weights = (e * (1.0 / jnp.sum(e, axis=-1, keepdims=True))).astype(BF)
         return dot(weights, jnp.where(keep, v, 0))
 
     def attend(l, c):

time: 111 us -> 111 us (level)
  no operation moved by 1% of the time
where the time goes in v4:
time: 111 us; the launch traced here: 110 us
  Pallas kernels  106 us (95%)
  local copies, waits for them, and re-layouts  3.97 us (4%)
    pallas_call x1, Pallas kernels, per_device(): pl.pallas_call(kernel, out_shape=jax.ShapeDtypeStruct((768, 2048), BF), i...  106 us
    unnamed x1, local copies, waits for them, and re-layouts  3.97 us

profile of v4, /device:TPU:4, one launch (start us, length us, event | category | flops | bytes accessed | tf_op | source)
XLA Modules:
  0.0 110.2 jit_solution(3295643240754114496)
XLA Ops:
  0.0 106.2 %encode.1 = bf16[768,2048]{1,0:T(8,128)(2,1)} custom-call(bf16[256,1280]{1,0:T(8,128)(2,1)} %audio_ref.1, bf16[256,1280]{1,0:T(8,128)(2,1)} %vision_ref.1, s32[1,256]{1,0:T(1,128)} %ids_a_ref.1, s32[1,256]{1,0:T(1,128)} %ids_v_ref.1, s32[1,768]{1,0:T(1,128)} %order_ref.1, bf16[768,2048]{1,0:T(8,128)(2,1)} %text_ref.1, bf16[1,1280]{1,0:T(2,128)(2,1)} %gain_ref.1, ...), custom_call_target="tpu_custom_call" | custom-call | flops 12000000000 | bytes 30000000 | tf_op jit(solution)/shard_map/encode/pallas_call | solution.py:608
  106.2 4.0 %copy.12 = bf16[768,2048]{1,0:T(8,128)(2,1)} copy(bf16[768,2048]{1,0:T(8,128)(2,1)} %encode.1) | data formatting | bytes 6291456
